TPU v7x, 32 devices: a whole 2x2x4 slice. The times are simulated.
32 devices in a mesh: dp: 4 (over y, x), ctx: 2 (over core), head: 4 (over z).
Axes of the slice: x: 2, y: 2, z: 4, core: 2. Of those that a mesh axis runs over, the one named last changes fastest.
Arguments:
- hidden: bfloat16 [8192, 768], P(('dp', 'ctx', 'head')), may hold values from -6 to 6
- norm_gain: float32 [768], replicated, may hold values from 0.5 to 1.5
- in_weight: bfloat16 [768, 3352], P(('dp', 'ctx')), may hold values from -0.21875 to 0.21875
- conv_weight: float32 [4, 1792], replicated, may hold values from -1.75 to 1.75
- conv_bias: float32 [1792], replicated, may hold values from -1.5 to 1.5
- dt_bias: float32 [24], replicated, may hold values from -6 to -2.5
- a_log: float32 [24], replicated, may hold values from -4.6 to 1.6
- skip_gain: float32 [24], replicated, may hold values from 0.5 to 2
- gate_gain: float32 [1536], replicated, may hold values from 0.5 to 1.5
- out_weight: bfloat16 [1536, 768], P(('dp', 'ctx')), may hold values from -0.15625 to 0.15625
- cotangent: bfloat16 [8192, 768], P(('dp', 'ctx', 'head')), may hold values from -6 to 6
Outputs:
- output: bfloat16 [8192, 768], P(('dp', 'ctx', 'head'))
- grad_hidden: float32 [8192, 768], P(('dp', 'ctx', 'head'))
- grad_norm_gain: float32 [768], replicated
- grad_in_weight: float32 [768, 3352], P(('dp', 'ctx'))
- grad_conv_weight: float32 [4, 1792], replicated
- grad_conv_bias: float32 [1792], replicated
- grad_dt_bias: float32 [24], replicated
- grad_a_log: float32 [24], replicated
- grad_skip_gain: float32 [24], replicated
- grad_gate_gain: float32 [1536], replicated
- grad_out_weight: float32 [1536, 768], P(('dp', 'ctx'))
All inputs are finite; a program needn't handle non-finite values.
Results may differ from a plain program's by a relative error of at most 0.0095.
The roundings to bfloat16 on the way count: a program that leaves them out, or rounds other values in their place, can miss the bound.
Values may be sent and summed in bfloat16 or wider, within the bound.
A program may use at most 128 MiB of HBM per device.

v0:
```python
import jax
import jax.numpy as jnp
from jax import lax
from jax.sharding import PartitionSpec as P

HEADS = 24
HEADDIM = 64
STATE = 128
CONV = 4
BLOCK = 256
INNER = 1536
CONV_CH = 1792


epsilon = 1e-05
highest = lax.Precision.HIGHEST


def shifted(value, axis, by):
    length = lax.axis_size(axis)
    pairs = [(i, i + by) for i in range(length) if 0 <= i + by < length]
    return lax.ppermute(value, axis, pairs)


def prefix(part, axis, combine, identity, reverse):
    count = lax.axis_size(axis)
    place = lax.axis_index(axis)
    ahead = count - 1 - place if reverse else place
    gathered = jax.tree.map(lambda a: lax.all_gather(a, axis), part)
    state = jax.tree.map(lambda a, e: jnp.zeros_like(a) + jnp.asarray(e, a.dtype), part, identity)

    def one(hop, state):
        source = count - 1 - hop if reverse else hop
        return combine(
            state, jax.tree.map(lambda a: lax.dynamic_index_in_dim(a, source, 0, False), gathered)
        )

    return lax.fori_loop(0, ahead, one, state)


def rms_scale(values, gain_vec):
    variance = jnp.mean(values * values, axis=-1, keepdims=True)
    return values * lax.rsqrt(variance + epsilon) * gain_vec


def gated_norm(mixer_out, gate_part, gain_vec):
    return rms_scale(mixer_out * jax.nn.silu(gate_part), gain_vec)


def conv_silu(extended, conv_w, conv_b):
    rows_out = extended.shape[0] - (CONV - 1)
    total = conv_b + conv_w[0] * extended[0:rows_out]
    for offset in range(1, CONV):
        total = total + conv_w[offset] * extended[offset : offset + rows_out]
    return jax.nn.silu(total)


def block_math(carry_state, pieces):
    inputs, b_rows, c_rows, step_sizes, log_decay = pieces
    cumulative = jnp.cumsum(log_decay, axis=0)
    length = inputs.shape[0]
    row_ids = lax.broadcasted_iota(jnp.int32, (length, length), 0)
    col_ids = lax.broadcasted_iota(jnp.int32, (length, length), 1)
    causal = (col_ids <= row_ids)[None]
    spread = cumulative.T[:, :, None] - cumulative.T[:, None, :]
    safe_spread = jnp.where(causal, spread, jnp.zeros_like(spread))
    decays = jnp.where(causal, jnp.exp(safe_spread), jnp.zeros_like(spread))
    scores = jnp.dot(c_rows, b_rows.T, precision=highest)
    weighted = inputs * step_sizes[:, :, None]
    inner_part = jnp.einsum("hij,jhp->ihp", decays * scores[None], weighted, precision=highest)
    carried = jnp.exp(cumulative)[:, :, None] * jnp.einsum(
        "in,hpn->ihp", c_rows, carry_state, precision=highest
    )
    last_sum = cumulative[-1]
    tail_decay = jnp.exp(last_sum[None, :] - cumulative)
    new_state = jnp.exp(last_sum)[:, None, None] * carry_state + jnp.einsum(
        "jh,jhp,jn->hpn", tail_decay, weighted, b_rows, precision=highest
    )
    return (new_state, inner_part + carried)


def decay_logs(dt_rows, bias_local, rate_local):
    step_sizes = jax.nn.softplus(dt_rows + bias_local)
    return (step_sizes, -step_sizes * jnp.exp(rate_local))


def segment_scan(x_heads, b_rows, c_rows, dt_rows, bias_local, rate_local, skip_local, first_state):
    step_sizes, log_decay = decay_logs(dt_rows, bias_local, rate_local)
    seg_rows, head_count, head_width = x_heads.shape
    block_count = seg_rows // BLOCK
    pieces = (
        x_heads.reshape(block_count, BLOCK, head_count, head_width),
        b_rows.reshape(block_count, BLOCK, STATE),
        c_rows.reshape(block_count, BLOCK, STATE),
        step_sizes.reshape(block_count, BLOCK, head_count),
        log_decay.reshape(block_count, BLOCK, head_count),
    )
    last_state, outputs = lax.scan(block_math, first_state, pieces)
    mixer_out = (
        outputs.reshape(seg_rows, head_count, head_width) + skip_local[None, :, None] * x_heads
    )
    return (mixer_out, last_state)


def link_states(earlier, later):
    return (earlier[0] + later[0], jnp.exp(later[0])[:, None, None] * earlier[1] + later[1])


def place_heads(local_vals, head_first):
    return lax.dynamic_update_slice_in_dim(
        jnp.zeros((HEADS,), jnp.float32), local_vals, head_first, 0
    )


def body(
    hidden,
    norm_gain,
    in_weight,
    conv_weight,
    conv_bias,
    dt_bias,
    a_log,
    skip_gain,
    gate_gain,
    out_weight,
    cotangent,
):
    gathered_in, gathered_out = (
        lax.all_gather(in_weight, ("dp", "ctx"), axis=0, tiled=True),
        lax.all_gather(out_weight, ("dp", "ctx"), axis=0, tiled=True),
    )
    tok_rows = hidden.shape[0]
    head_groups = lax.axis_size("head")
    local_heads = HEADS // head_groups
    hidden_f = hidden.astype(jnp.float32)
    normed_low = rms_scale(hidden_f, norm_gain).astype(jnp.bfloat16)
    projected = jnp.dot(normed_low, gathered_in, preferred_element_type=jnp.float32).astype(
        jnp.bfloat16
    )
    gate_part = projected[:, :INNER]
    conv_in = projected[:, INNER : INNER + CONV_CH]
    dt_raw = projected[:, INNER + CONV_CH :]
    earlier_rows = shifted(conv_in[tok_rows - (CONV - 1) :], ("ctx", "head"), 1)
    extended = jnp.concatenate([earlier_rows, conv_in], axis=0).astype(jnp.float32)
    activated = conv_silu(extended, conv_weight, conv_bias).astype(jnp.bfloat16)
    x_sent, dt_heads, bc_heads = (
        lax.all_to_all(activated[:, :INNER], "head", split_axis=1, concat_axis=0, tiled=True),
        lax.all_to_all(dt_raw, "head", split_axis=1, concat_axis=0, tiled=True),
        lax.all_to_all(
            jnp.tile(activated[:, INNER:], (1, head_groups)),
            "head",
            split_axis=1,
            concat_axis=0,
            tiled=True,
        ),
    )
    seg_rows = x_sent.shape[0]
    x_heads = x_sent.astype(jnp.float32).reshape(seg_rows, local_heads, HEADDIM)
    b_rows = bc_heads[:, :STATE].astype(jnp.float32)
    c_rows = bc_heads[:, STATE:].astype(jnp.float32)
    dt_rows = dt_heads.astype(jnp.float32)
    head_first = lax.axis_index("head") * local_heads
    bias_local = lax.dynamic_slice_in_dim(dt_bias, head_first, local_heads)
    rate_local = lax.dynamic_slice_in_dim(a_log, head_first, local_heads)
    skip_local = lax.dynamic_slice_in_dim(skip_gain, head_first, local_heads)
    zero_state = jnp.zeros((local_heads, HEADDIM, STATE), jnp.float32)
    local_out, local_state = segment_scan(
        x_heads, b_rows, c_rows, dt_rows, bias_local, rate_local, skip_local, zero_state
    )
    step_sizes, log_decay = decay_logs(dt_rows, bias_local, rate_local)
    segment_log = jnp.sum(log_decay, axis=0)
    running_log = jnp.cumsum(log_decay, axis=0)
    identity = (jnp.zeros((local_heads,), jnp.float32), zero_state)
    arrived_log, arrived_state = prefix(
        (segment_log, local_state), "ctx", link_states, identity, False
    )
    carried = jnp.exp(running_log)[:, :, None] * jnp.einsum(
        "tn,hpn->thp", c_rows, arrived_state, precision=highest
    )
    mixer_heads = (
        (local_out + carried).reshape(seg_rows, local_heads * HEADDIM).astype(jnp.bfloat16)
    )
    mixer_tok = lax.all_to_all(mixer_heads, "head", split_axis=0, concat_axis=1, tiled=True)
    gate_f = gate_part.astype(jnp.float32)
    mixer_f = mixer_tok.astype(jnp.float32)
    gated_low = gated_norm(mixer_f, gate_f, gate_gain).astype(jnp.bfloat16)
    branch = jnp.dot(gated_low, gathered_out, preferred_element_type=jnp.float32)
    output = (hidden_f + branch).astype(jnp.bfloat16)
    weight_in, weight_out = (
        lax.all_gather(in_weight, ("dp", "ctx"), axis=0, tiled=True),
        lax.all_gather(out_weight, ("dp", "ctx"), axis=0, tiled=True),
    )
    grad_out_part = jnp.einsum(
        "ti,td->id", gated_low, cotangent, preferred_element_type=jnp.float32
    )
    grad_gated = jnp.einsum("td,id->ti", cotangent, weight_out, preferred_element_type=jnp.float32)
    gated_value, gated_pull = jax.vjp(gated_norm, mixer_f, gate_f, gate_gain)
    grad_mixer, grad_gate, grad_ggain = gated_pull(grad_gated)
    mixer_grad_heads = lax.all_to_all(
        grad_mixer.astype(jnp.bfloat16), "head", split_axis=1, concat_axis=0, tiled=True
    )
    grad_heads = mixer_grad_heads.astype(jnp.float32).reshape(seg_rows, local_heads, HEADDIM)
    from_output = jnp.einsum(
        "th,thp,tn->hpn", jnp.exp(running_log), grad_heads, c_rows, precision=highest
    )
    later_log, later_grad = prefix((segment_log, from_output), "ctx", link_states, identity, True)
    segment_value, segment_pull = jax.vjp(
        segment_scan,
        x_heads,
        b_rows,
        c_rows,
        dt_rows,
        bias_local,
        rate_local,
        skip_local,
        arrived_state,
    )
    grad_parts = segment_pull((grad_heads, later_grad))
    grad_x = grad_parts[0].reshape(seg_rows, local_heads * HEADDIM).astype(jnp.bfloat16)
    grad_dt = grad_parts[3].astype(jnp.bfloat16)
    grad_x_tok, grad_dt_tok = (
        lax.all_to_all(grad_x, "head", split_axis=0, concat_axis=1, tiled=True),
        lax.all_to_all(grad_dt, "head", split_axis=0, concat_axis=1, tiled=True),
    )
    grad_bc_tok = lax.psum_scatter(
        jnp.concatenate([grad_parts[1], grad_parts[2]], axis=1).astype(jnp.bfloat16),
        "head",
        scatter_dimension=0,
        tiled=True,
    )
    grad_bc_low = lax.optimization_barrier(grad_bc_tok).astype(jnp.float32)
    grad_act = jnp.concatenate([grad_x_tok.astype(jnp.float32), grad_bc_low], axis=1)
    conv_value, conv_pull = jax.vjp(conv_silu, extended, conv_weight, conv_bias)
    grad_ext, grad_cw, grad_cb = conv_pull(grad_act)
    later_rows = shifted(grad_ext[: CONV - 1], ("ctx", "head"), -1)
    grad_conv_in = grad_ext[CONV - 1 :].at[tok_rows - (CONV - 1) :].add(later_rows)
    grad_proj = jnp.concatenate(
        [grad_gate, grad_conv_in, grad_dt_tok.astype(jnp.float32)], axis=1
    ).astype(jnp.bfloat16)
    grad_in_part = jnp.einsum(
        "td,tp->dp", normed_low, grad_proj, preferred_element_type=jnp.float32
    )
    grad_normed = jnp.einsum("tp,dp->td", grad_proj, weight_in, preferred_element_type=jnp.float32)
    norm_value, norm_pull = jax.vjp(rms_scale, hidden_f, norm_gain)
    grad_hidden_part, grad_ngain = norm_pull(grad_normed)
    grad_hidden = cotangent.astype(jnp.float32) + grad_hidden_part
    grad_in_shard, grad_out_shard = (
        lax.psum_scatter(grad_in_part, ("dp", "ctx"), scatter_dimension=0, tiled=True),
        lax.psum_scatter(grad_out_part, ("dp", "ctx"), scatter_dimension=0, tiled=True),
    )
    grad_in_weight, grad_out_weight = lax.psum((grad_in_shard, grad_out_shard), "head")
    small_sums = lax.psum(
        (
            grad_ngain,
            grad_cw,
            grad_cb,
            place_heads(grad_parts[4], head_first),
            place_heads(grad_parts[5], head_first),
            place_heads(grad_parts[6], head_first),
            grad_ggain,
        ),
        ("dp", "ctx", "head"),
    )
    return (
        output,
        grad_hidden,
        small_sums[0],
        grad_in_weight,
        small_sums[1],
        small_sums[2],
        small_sums[3],
        small_sums[4],
        small_sums[5],
        small_sums[6],
        grad_out_weight,
    )


def solution(mesh):
    return jax.shard_map(
        body,
        mesh=mesh,
        in_specs=(
            P(("dp", "ctx", "head"), None),
            P(),
            P(("dp", "ctx"), None),
            P(),
            P(),
            P(),
            P(),
            P(),
            P(),
            P(("dp", "ctx"), None),
            P(("dp", "ctx", "head"), None),
        ),
        out_specs=(
            P(("dp", "ctx", "head"), None),
            P(("dp", "ctx", "head"), None),
            P(),
            P(("dp", "ctx"), None),
            P(),
            P(),
            P(),
            P(),
            P(),
            P(),
            P(("dp", "ctx"), None),
        ),
        check_vma=False,
    )
```

profile of v0, /device:TPU:0, one launch (start us, length us, event | category | flops | bytes accessed | tf_op | source)
XLA Modules:
  0.0 793.6 jit_solution(16151625462681672357)
XLA Ops:
  9.1 44.9 %all-gather.6.cloned.1.call-done = bf16[768,3352]{1,0:T(8,128)(2,1)} async-done(((bf16[96,3352]{1,0:T(8,128)(2,1)}), bf16[768,3352]{1,0:T(8,128)(2,1)}) %all-gather.6.cloned.1.call-update) | async-done | bytes 5148688 | tf_op jit(solution)/shard_map/all_gather | solution.py:129
  54.0 4.9 convolution_convert_fusion
  67.9 4.9 collective-permute-done
  80.3 5.6 all-to-all-start.2
  88.0 11.8 %all-to-all-done.2 = bf16[256,4,256]{2,0,1:T(8,128)(2,1)S(1)} async-done(((bf16[256,4,256]{2,0,1:T(8,128)(2,1)}), bf16[256,4,256]{2,0,1:T(8,128)(2,1)S(1)}, u32[]{:S(2)}, u32[]{:S(2)}) %all-to-all-start.2) | async-done | bytes 524320 | tf_op jit(solution)/shard_map/all_to_all | solution.py:149
  115.3 8.5 %all-to-all-done.1 = bf16[256,4,384]{0,2,1:T(8,128)(2,1)} async-done(((bf16[256,4,384]{0,2,1:T(8,128)(2,1)}), bf16[256,4,384]{0,2,1:T(8,128)(2,1)}, u32[]{:S(2)}, u32[]{:S(2)}) %all-to-all-start.1) | async-done | bytes 786464 | tf_op jit(solution)/shard_map/all_to_all | solution.py:147
  126.8 81.8 %while.114 = (s32[]{:T(128)}, f32[6,64,128]{2,1,0:T(8,128)S(1)}, f32[4,256,6,64]{1,0,3,2:T(4,128)}, f32[4,256,6]{1,2,0:T(8,128)}, f32[4,256,6,64]{1,3,2,0:T(8,12...) while((s32[]{:T(128)}, f32[6,64,128]{2,1,0:T(8,128)S(1)}, ...), condition=%wide.region_4.5_spmd.clone, body=%wide.region_1.4_spmd.clone.sunk | while | flops 707167744 | bytes 5447488 | solution.py:98
  136.2 9.5 %dynamic_update_slice.227 = f32[4,256,6,64]{1,0,3,2:T(4,128)} dynamic-update-slice(f32[4,256,6,64]{1,0,3,2:T(4,128)} %get-tuple-element.2244, f32[1,256,6,64]{1,0,3,2:T(1,128)S(1)} %copy.300, s32[]{:T(128)} %get-tuple-element.2242, s32[]{:T(128)} %constant.263.clone.1..sunk.3, s32[]{:T(128)} %constant.263.clone.1..sunk.3, s32[]{:T(128)} %constant.263.clone.1..sunk.3) | dynamic-update-slice | bytes 786436 | tf_op jit(solution)/shard_map/while/body/jit(dynamic_update_index_in_dim)/dynamic_update_slice | solution.py:98
  156.6 9.5 %dynamic_update_slice.227 = f32[4,256,6,64]{1,0,3,2:T(4,128)} dynamic-update-slice(f32[4,256,6,64]{1,0,3,2:T(4,128)} %get-tuple-element.2244, f32[1,256,6,64]{1,0,3,2:T(1,128)S(1)} %copy.300, s32[]{:T(128)} %get-tuple-element.2242, s32[]{:T(128)} %constant.263.clone.1..sunk.3, s32[]{:T(128)} %constant.263.clone.1..sunk.3, s32[]{:T(128)} %constant.263.clone.1..sunk.3) | dynamic-update-slice | bytes 786436 | tf_op jit(solution)/shard_map/while/body/jit(dynamic_update_index_in_dim)/dynamic_update_slice | solution.py:98
  177.1 9.5 %dynamic_update_slice.227 = f32[4,256,6,64]{1,0,3,2:T(4,128)} dynamic-update-slice(f32[4,256,6,64]{1,0,3,2:T(4,128)} %get-tuple-element.2244, f32[1,256,6,64]{1,0,3,2:T(1,128)S(1)} %copy.300, s32[]{:T(128)} %get-tuple-element.2242, s32[]{:T(128)} %constant.263.clone.1..sunk.3, s32[]{:T(128)} %constant.263.clone.1..sunk.3, s32[]{:T(128)} %constant.263.clone.1..sunk.3) | dynamic-update-slice | bytes 786436 | tf_op jit(solution)/shard_map/while/body/jit(dynamic_update_index_in_dim)/dynamic_update_slice | solution.py:98
  197.5 9.5 %dynamic_update_slice.227 = f32[4,256,6,64]{1,0,3,2:T(4,128)} dynamic-update-slice(f32[4,256,6,64]{1,0,3,2:T(4,128)} %get-tuple-element.2244, f32[1,256,6,64]{1,0,3,2:T(1,128)S(1)} %copy.300, s32[]{:T(128)} %get-tuple-element.2242, s32[]{:T(128)} %constant.263.clone.1..sunk.3, s32[]{:T(128)} %constant.263.clone.1..sunk.3, s32[]{:T(128)} %constant.263.clone.1..sunk.3) | dynamic-update-slice | bytes 786436 | tf_op jit(solution)/shard_map/while/body/jit(dynamic_update_index_in_dim)/dynamic_update_slice | solution.py:98
  229.3 4.5 all-to-all-start.3
  233.9 20.6 %all-to-all-done.3 = bf16[4,256,384]{1,2,0:T(8,128)(2,1)} async-done(((bf16[4,256,384]{1,2,0:T(8,128)(2,1)}), bf16[4,256,384]{1,2,0:T(8,128)(2,1)}, u32[]{:S(2)}, u32[]{:S(2)}) %all-to-all-start.3) | async-done | bytes 786464 | tf_op jit(solution)/shard_map/all_to_all | solution.py:183
  274.6 91.9 %while.112 = (s32[]{:T(128)}, f32[6,64,128]{2,1,0:T(8,128)S(1)}, f32[4,6,256,256]{3,2,1,0:T(8,128)}, f32[4,128,256]{1,2,0:T(8,128)}, f32[4,256,6,1]{1,2,3,0:T(8,...) while((s32[]{:T(128)}, f32[6,64,128]{2,1,0:T(8,128)S(1)}, ...), condition=%wide.region_17.18_spmd.clone.clone, body=%wide.region_14.17_spmd.clone.clone.sunk | while | flops 405014016 | bytes 9591437 | solution.py:98
  383.3 142.3 %while.113 = (s32[]{:T(128)}, f32[6,64,128]{2,1,0:T(8,128)S(1)}, f32[4,256,6,64]{1,3,2,0:T(8,128)}, bf16[4,256,128]{2,1,0:T(8,128)(2,1)}, bf16[4,256,128]{2,1,0:...) while((s32[]{:T(128)}, f32[6,64,128]{2,1,0:T(8,128)S(1)}, ...), condition=%wide.region_28.29_spmd.clone.clone, body=%wide.region_18.28_spmd.clone.clone.sunk | while | flops 1413914112 | bytes 15158465 | solution.py:98
  399.1 7.6 reduce-window.72
  434.8 7.6 reduce-window.72
  470.3 7.6 reduce-window.72
  505.9 7.6 reduce-window.72
  530.5 4.5 fusion.172
  538.6 5.0 all-to-all-start.5
  543.7 12.0 %reduce-scatter.4.cloned.1.call-done = bf16[256,256]{0,1:T(8,128)(2,1)} async-done(((bf16[1024,256]{0,1:T(8,128)(2,1)}), bf16[256,256]{0,1:T(8,128)(2,1)}) %reduce-scatter.4.cloned.1.call-update) | async-done | bytes 131088 | tf_op jit(solution)/shard_map/reduce_scatter | solution.py:225
  555.7 10.5 %all-to-all-done.5 = bf16[4,256,384]{1,2,0:T(8,128)(2,1)} async-done(((bf16[4,256,384]{1,2,0:T(8,128)(2,1)}), bf16[4,256,384]{1,2,0:T(8,128)(2,1)}, u32[]{:S(2)}, u32[]{:S(2)}) %all-to-all-start.5) | async-done | bytes 786464 | tf_op jit(solution)/shard_map/all_to_all | solution.py:222
  566.2 5.2 multiply_reduce_fusion.4
  580.3 9.5 %all_to_all.85 = bf16[4,256,6]{1,2,0:T(8,128)(2,1)S(1)} all-to-all(bf16[4,256,6]{1,2,0:T(8,128)(2,1)S(1)} %get-tuple-element.1697), channel_id=1, replica_groups=mesh['dp'=4,'ctx'=2,'head'=4] {'head'}, dimensions={0} | all-to-all | bytes 24576 | tf_op jit(solution)/shard_map/all_to_all | solution.py:223
  595.0 6.0 scatter-add.4
  601.0 7.3 fusion.150
  608.3 4.5 reduce-scatter.8.cloned.1.call-done
  612.9 86.0 %reduce-scatter.6.cloned.1.call-done = f32[96,3352]{1,0:T(8,128)} async-done(((f32[768,3352]{1,0:T(8,128)}), f32[96,3352]{1,0:T(8,128)}) %reduce-scatter.6.cloned.1.call-update) | async-done | bytes 1287184 | tf_op jit(solution)/shard_map/reduce_scatter | solution.py:248
  705.2 4.6 fusion.145
  709.8 43.0 %all-reduce.10 = (f32[768]{0:T(1024)}, f32[4,1792]{1,0:T(4,128)}, f32[1792]{0:T(1024)}, f32[24]{0:T(128)}, f32[24]{0:T(128)}, /*index=5*/f32[24]{0:T(128)}, f32[1536]{0:T(1024)}) all-reduce(f32[768]{0:T(1024)S(1)} %get-tuple-element.1543, ...), channel_id=1, replica_groups=mesh['dp'=4,'ctx'=2,'head'=4] {'dp','ctx','head'}, use_global_device_ids=true, to_apply=%region_32.33 | all-reduce | flops 11336 | bytes 90688 | tf_op jit(solution)/shard_map/psum | solution.py:252
  754.0 29.2 %all-reduce.14.cloned.1.call-done = (f32[96,3352]{1,0:T(8,128)}, f32[192,768]{1,0:T(8,128)}) async-done(((f32[96,3352]{1,0:T(8,128)}, f32[192,768]{1,0:T(8,128)}), (f32[96,3352]{1,0:T(8,128)}, f32[192,768]{1,0:T(8,128)})) %all-reduce.14.cloned.1.call-update) | async-done | bytes 1877008 | tf_op jit(solution)/shard_map/psum | solution.py:251
  (571 shorter events, 376.1 us)
Async XLA Ops:
  7.2 46.8 %all-gather.6.cloned.1.call-start = ((), (), s32[]{:S(2)}) async-start(), calls=%async_computation.10 | async-start | bytes 5971968 | tf_op jit(solution)/shard_map/all_gather | solution.py:129
  9.1 45.0 %copy-start.41 = (f32[256]{0:T(256)}, f32[256]{0:T(256)S(1)}, u32[]{:S(2)}) copy-start(f32[256]{0:T(256)S(1)} %fusion.147) | copy-start | bytes 3076
  9.1 44.9 %copy-start.38 = (f32[256]{0:T(256)}, f32[256]{0:T(256)S(1)}, u32[]{:S(2)}) copy-start(f32[256]{0:T(256)S(1)} %fusion.166) | copy-start | bytes 3076
  9.1 53.4 %copy-start.37 = (f32[4,1792]{1,0:T(4,128)S(1)}, f32[4,1792]{1,0:T(4,128)}, u32[]{:S(2)}) copy-start(f32[4,1792]{1,0:T(4,128)} %param.26) | copy-start | bytes 86020
  59.1 13.7 %collective-permute-start = (bf16[3,1792]{0,1:T(8,128)(2,1)S(1)}, bf16[3,1792]{0,1:T(8,128)(2,1)S(1)}, u32[]{:S(2)}, u32[]{:S(2)}) collective-permute-start(bf16[3,1792]{0,1:T(8,128)(2,1)S(1)} %slice.166), channel_id=1, source_target_pairs={{0,1},{1,2},{2,3},{3,4},{4,5},{5,6},{6,7},{8,9},{9,10},{10,11},{11... | collective-permute-start | bytes 32264 | tf_op jit(solution)/shard_map/ppermute | solution.py:22
  62.6 12.0 %copy-start.20 = (f32[1792]{0:T(1024)}, f32[1792]{0:T(1024)S(1)}, u32[]{:S(2)}) copy-start(f32[1792]{0:T(1024)S(1)} %get-tuple-element.1545) | copy-start | bytes 21508
  62.6 12.0 %copy-start.22 = (f32[1792]{0:T(1024)}, f32[1792]{0:T(1024)S(1)}, u32[]{:S(2)}) copy-start(f32[1792]{0:T(1024)S(1)} %get-tuple-element.1546) | copy-start | bytes 21508
  62.6 12.0 %copy-start.24 = (f32[1792]{0:T(1024)}, f32[1792]{0:T(1024)S(1)}, u32[]{:S(2)}) copy-start(f32[1792]{0:T(1024)S(1)} %get-tuple-element.1547) | copy-start | bytes 21508
  62.7 12.0 %copy-start.26 = (f32[1792]{0:T(1024)}, f32[1792]{0:T(1024)S(1)}, u32[]{:S(2)}) copy-start(f32[1792]{0:T(1024)S(1)} %get-tuple-element.1548) | copy-start | bytes 21508
  64.3 15.2 %all-to-all-start = ((bf16[256,4,6]{0,2,1:T(8,128)(2,1)}), bf16[256,4,6]{0,2,1:T(8,128)(2,1)S(1)}, u32[]{:S(2)}, u32[]{:S(2)}) async-start(bf16[256,4,6]{0,2,1:T(8,128)(2,1)} %all_to_all.31), calls=%async_computation | async-start | bytes 32768 | tf_op jit(solution)/shard_map/all_to_all | solution.py:148
  79.5 31.8 %copy-start.15 = (bf16[256,4,6]{0,2,1:T(8,128)(2,1)}, bf16[256,4,6]{0,2,1:T(8,128)(2,1)S(1)}, u32[]{:S(2)}) copy-start(bf16[256,4,6]{0,2,1:T(8,128)(2,1)S(1)} %all-to-all-done) | copy-start | bytes 36868
  80.3 19.6 %all-to-all-start.2 = ((bf16[256,4,256]{2,0,1:T(8,128)(2,1)}), bf16[256,4,256]{2,0,1:T(8,128)(2,1)S(1)}, u32[]{:S(2)}, u32[]{:S(2)}) async-start(bf16[256,4,256]{2,0,1:T(8,128)(2,1)} %tile.2), calls=%async_computation.2 | async-start | bytes 1048576 | tf_op jit(solution)/shard_map/all_to_all | solution.py:149
  85.9 19.0 %copy-start.54 = (f32[24]{0:T(128)S(1)}, f32[24]{0:T(128)}, u32[]{:S(2)}) copy-start(f32[24]{0:T(128)} %param.28) | copy-start | bytes 292
  85.9 19.0 %copy-start.58 = (u32[32]{0:T(128)S(1)}, u32[32]{0:T(128)}, u32[]{:S(2)}) copy-start(u32[32]{0:T(128)} %constant.298) | copy-start | bytes 388
  85.9 20.3 %copy-start.52 = (f32[24]{0:T(128)S(1)}, f32[24]{0:T(128)}, u32[]{:S(2)}) copy-start(f32[24]{0:T(128)} %param.29) | copy-start | bytes 292
  85.9 21.4 %copy-start.55 = (f32[24]{0:T(128)S(1)}, f32[24]{0:T(128)}, u32[]{:S(2)}) copy-start(f32[24]{0:T(128)} %param.30) | copy-start | bytes 292
  99.9 13.7 %copy-start.4 = (bf16[256,4,256]{2,0,1:T(8,128)(2,1)}, bf16[256,4,256]{2,0,1:T(8,128)(2,1)S(1)}, u32[]{:S(2)}) copy-start(bf16[256,4,256]{2,0,1:T(8,128)(2,1)S(1)} %all-to-all-done.2) | copy-start | bytes 1572868
  99.9 23.9 %all-to-all-start.1 = ((bf16[256,4,384]{0,2,1:T(8,128)(2,1)}), bf16[256,4,384]{0,2,1:T(8,128)(2,1)}, u32[]{:S(2)}, u32[]{:S(2)}) async-start(bf16[256,4,384]{0,2,1:T(8,128)(2,1)} %bitcast.560), calls=%async_computation.1 | async-start | bytes 1572864 | tf_op jit(solution)/shard_map/all_to_all | solution.py:147
  104.1 153.5 %all-gather.8.cloned.1.call-start = ((), (), s32[]{:S(2)}) async-start(), calls=%async_computation.11 | async-start | bytes 2654208 | tf_op jit(solution)/shard_map/all_gather | solution.py:130
  113.6 106.6 %copy-start.13 = (f32[1,6,8,128]{3,1,2,0:T(8,128)}, f32[1,6,8,128]{3,1,2,0:T(8,128)S(1)}, u32[]{:S(2)}) copy-start(f32[1,6,8,128]{3,1,2,0:T(8,128)S(1)} %copy.261) | copy-start | bytes 73732
  229.3 25.2 %all-to-all-start.3 = ((bf16[4,256,384]{1,2,0:T(8,128)(2,1)}), bf16[4,256,384]{1,2,0:T(8,128)(2,1)}, u32[]{:S(2)}, u32[]{:S(2)}) async-start(bf16[4,256,384]{1,2,0:T(8,128)(2,1)} %copy.184), calls=%async_computation.3 | async-start | bytes 1572864 | tf_op jit(solution)/shard_map/all_to_all | solution.py:183
  233.9 23.7 %copy-start.8 = (bf16[256,768]{1,0:T(8,128)(2,1)S(1)}, bf16[256,768]{1,0:T(8,128)(2,1)}, u32[]{:S(2)}) copy-start(bf16[256,768]{1,0:T(8,128)(2,1)} %param.33) | copy-start | bytes 1179652
  233.9 23.7 %copy-start.17 = (f32[1536]{0:T(1024)S(1)}, f32[1536]{0:T(1024)}, u32[]{:S(2)}) copy-start(f32[1536]{0:T(1024)} %param.31) | copy-start | bytes 18436
  265.0 101.5 %all-to-all-start.4 = ((bf16[256,4,384]{0,2,1:T(8,128)(2,1)}), bf16[256,4,384]{0,2,1:T(8,128)(2,1)}, u32[]{:S(2)}, u32[]{:S(2)}) async-start(bf16[256,4,384]{0,2,1:T(8,128)(2,1)} %bitcast.561), calls=%async_computation.4 | async-start | bytes 1572864 | tf_op jit(solution)/shard_map/all_to_all | solution.py:199
  269.3 286.5 %reduce-scatter.4.cloned.1.call-start = ((), (), s32[]{:S(2)}) async-start(), calls=%async_computation.12 | async-start | bytes 655360 | tf_op jit(solution)/shard_map/reduce_scatter | solution.py:225
  530.4 82.5 %reduce-scatter.8.cloned.1.call-start = ((), (), s32[]{:S(2)}) async-start(), calls=%async_computation.14 | async-start | bytes 5308416 | tf_op jit(solution)/shard_map/reduce_scatter | solution.py:249
  538.6 27.7 %all-to-all-start.5 = ((bf16[4,256,384]{1,2,0:T(8,128)(2,1)}), bf16[4,256,384]{1,2,0:T(8,128)(2,1)}, u32[]{:S(2)}, u32[]{:S(2)}) async-start(bf16[4,256,384]{1,2,0:T(8,128)(2,1)} %fusion.138), calls=%async_computation.5 | async-start | bytes 1572864 | tf_op jit(solution)/shard_map/all_to_all | solution.py:222
  543.6 155.2 %reduce-scatter.6.cloned.1.call-start = ((), (), s32[]{:S(2)}) async-start(), calls=%async_computation.13 | async-start | bytes 11943936 | tf_op jit(solution)/shard_map/reduce_scatter | solution.py:248
  577.4 14.2 %collective-permute-start.1 = (f32[3,1792]{1,0:T(4,128)S(1)}, f32[3,1792]{1,0:T(4,128)S(1)}, u32[]{:S(2)}, u32[]{:S(2)}) collective-permute-start(f32[3,1792]{1,0:T(4,128)S(1)} %copy.197), channel_id=1, source_target_pairs={{1,0},{2,1},{3,2},{4,3},{5,4},{6,5},{7,6},{9,8},{10,9},{11,10},{12... | collective-permute-start | bytes 64520 | tf_op jit(solution)/shard_map/ppermute | solution.py:22
  608.3 90.6 %copy-start.1 = (f32[256,1536]{0,1:T(8,128)S(1)}, f32[256,1536]{0,1:T(8,128)}, u32[]{:S(2)}) copy-start(f32[256,1536]{0,1:T(8,128)} %get-tuple-element.1700) | copy-start | bytes 4718596
  608.3 175.0 %all-reduce.14.cloned.1.call-start = ((), (), s32[]{:S(2)}) async-start(), calls=%async_computation.15 | async-start | bytes 3833856 | tf_op jit(solution)/shard_map/psum | solution.py:251
  705.2 47.7 %copy-start.42 = (f32[256]{0:T(256)S(1)}, f32[256]{0:T(256)}, u32[]{:S(2)}) copy-start(f32[256]{0:T(256)} %copy-done.41) | copy-start | bytes 3076
  (44 other events, 193.4 us)
Sparse Core Ops, SparseCore 0:
  9.9 44.0 all-gather.5
  106.8 29.4 all-gather.7
  530.5 25.1 reduce-scatter.3
  559.0 53.8 reduce-scatter.7
  616.6 82.1 reduce-scatter.5
  701.3 81.9 all-reduce.13
where the time goes:
time: 804 us; the launch traced here: 794 us
  waiting for transfers between devices  234 us (29%)
  local copies, waits for them, and re-layouts  165 us (21%)
  matrix products  160 us (20%)
  other arithmetic  125 us (16%)
  blocking collectives  59.3 us (7%)
  starting transfers between devices  32.2 us (4%)
  between operations  15.9 us (2%)
    reduce_scatter x1, waiting for transfers between devices, body(): lax.psum_scatter(grad_in_part, ('dp', 'ctx'), scatter_dimension=0, tiled=...  86 us
    dynamic_update_slice x52, local copies, waits for them, and re-layouts, segment_scan(): last_state, outputs = lax.scan(block_math, first_state, pieces)  74.6 us
    another operation x39, other arithmetic  53.8 us
    all_gather x1, waiting for transfers between devices, body(): lax.all_gather(in_weight, ('dp', 'ctx'), axis=0, tiled=True)  44.9 us
    psum x1, blocking collectives, body(): lax.psum((grad_ngain, grad_cw, grad_cb, place_heads(grad_parts[4], head_f...  43 us
    dot_general x12, matrix products, block_math(): jnp.einsum('hij,jhp->ihp', decays * scores[None], weighted, precision=hig...  42.2 us
    dot_general x16, matrix products, block_math(): scores = jnp.dot(c_rows, b_rows.T, precision=highest)  29.8 us
    psum x1, waiting for transfers between devices, body(): lax.psum((grad_in_shard, grad_out_shard), 'head')  29.2 us
  transfers between devices with their start and end apart: 14, of which 10 were waited for; matrix products, arithmetic and copies ran while one was open for 34% of the time, Pallas kernels for 0%

commit v1 on v0

v1 whole, which is shorter than its diff:
```python
import jax
import jax.numpy as jnp
from jax import lax
from jax.experimental import pallas as pl
from jax.experimental.pallas import tpu as pltpu
from jax.sharding import PartitionSpec as P

HEADS = 24
HEADDIM = 64
STATE = 128
CONV = 4
INNER = 1536
CONV_CH = 1792
PAIRS = HEADS // 2
PAIR = 2 * HEADDIM
HALO = 8

epsilon = 1e-05
highest = lax.Precision.HIGHEST
f32 = jnp.float32
bf16 = jnp.bfloat16
WEIGHT_AXES = ("dp", "ctx")
SEQ_AXES = ("ctx", "head")


def dot(a, b, dims=(1, 0), **more):
    return lax.dot_general(
        a, b, (((dims[0],), (dims[1],)), ((), ())), preferred_element_type=f32, **more
    )


def pair_columns(p):
    return slice(p * PAIR, (p + 1) * PAIR)


def low_lanes(rows):
    return lax.broadcasted_iota(jnp.int32, (rows, PAIR), 1) < HEADDIM


def spread_pair(values, p, first):
    return jnp.where(first, values[:, 2 * p : 2 * p + 1], values[:, 2 * p + 1 : 2 * p + 2])


def head_selector():
    rows = lax.broadcasted_iota(jnp.int32, (INNER, 128), 0) // HEADDIM
    cols = lax.broadcasted_iota(jnp.int32, (INNER, 128), 1)
    return (rows == cols).astype(f32)


def call(kernel, outs, *args):
    whole = pl.BlockSpec(memory_space=pltpu.VMEM)
    return pl.pallas_call(
        kernel,
        out_shape=[jax.ShapeDtypeStruct(s, d) for s, d in outs],
        in_specs=[whole] * len(args),
        out_specs=[whole] * len(outs),
        compiler_params=pltpu.CompilerParams(vmem_limit_bytes=48 * 1024 * 1024),
    )(*args)


def state_kernel(act, step, tail, xw_out, xs_out, state_out):
    rows = act.shape[0]
    first = low_lanes(rows)
    step_v, tail_v = step[...], tail[...]
    b_rows = act[:, INNER : INNER + STATE]
    for p in range(PAIRS):
        cols = pair_columns(p)
        weighted = act[:, cols].astype(f32) * spread_pair(step_v, p, first)
        xw_out[:, cols] = weighted.astype(bf16)
        tailed = (weighted * spread_pair(tail_v, p, first)).astype(bf16)
        xs_out[:, cols] = tailed
        state_out[cols, :] = dot(tailed, b_rows, (0, 0)).astype(bf16)


def decay_matrix(cum_v, cum_rows, h, causal):
    spread = cum_v[:, h : h + 1] - cum_rows[h : h + 1, :]
    return jnp.exp(jnp.where(causal, spread, -1e30))


def causal_mask(rows):
    return lax.broadcasted_iota(jnp.int32, (rows, rows), 1) <= lax.broadcasted_iota(
        jnp.int32, (rows, rows), 0
    )


def inner_kernel(act, xw, cum, cum_t, y_out):
    rows = act.shape[0]
    first = low_lanes(rows)
    causal = causal_mask(rows)
    scores = dot(act[:, INNER + STATE :], act[:, INNER : INNER + STATE], (1, 1))
    cum_v, cum_rows = cum[...], cum_t[...]
    for p in range(PAIRS):
        cols = pair_columns(p)
        both = []
        for h in (2 * p, 2 * p + 1):
            weights = (decay_matrix(cum_v, cum_rows, h, causal) * scores).astype(bf16)
            both.append(dot(weights, xw[:, cols]))
        y_out[:, cols] = jnp.where(first, both[0], both[1])


def middle_kernel(
    act, inner, carry, grown, skip, gate, gain, grad_gn,
    gated_low_out, grad_gate_out, g_out, adjoint_out, ggain_out, skip_out, row_out, dc_out,
    gated_s, ystate_s,
):
    rows = act.shape[0]
    first = low_lanes(rows)
    grown_v = grown[...]
    c_rows = act[:, INNER + STATE :]
    square = jnp.zeros((rows, 1), f32)
    inner_product = jnp.zeros((rows, 1), f32)
    for p in range(PAIRS):
        cols = pair_columns(p)
        ystate = dot(c_rows, carry[cols, :], (1, 1)) * spread_pair(grown_v, p, first)
        ystate_s[:, cols] = ystate
        mixer = (inner[:, cols] + ystate + skip[:, cols] * act[:, cols].astype(f32)).astype(bf16)
        gate_f = gate[:, cols].astype(f32)
        gated = mixer.astype(f32) * (gate_f * jax.nn.sigmoid(gate_f))
        gated_s[:, cols] = gated
        g_out[:, cols] = mixer
        square = square + jnp.sum(gated * gated, axis=1, keepdims=True)
        inner_product = inner_product + jnp.sum(
            grad_gn[:, cols] * gain[:, cols] * gated, axis=1, keepdims=True
        )
    scale = lax.rsqrt(square * (1.0 / INNER) + epsilon)
    pull = scale * scale * scale * (inner_product * (1.0 / INNER))
    dc_total = jnp.zeros((rows, STATE), f32)
    row_total = jnp.zeros((rows, 128), f32)
    head_col = lax.broadcasted_iota(jnp.int32, (rows, 128), 1)
    for p in range(PAIRS):
        cols = pair_columns(p)
        gated = gated_s[:, cols]
        normal = gated * scale
        gated_low_out[:, cols] = (normal * gain[:, cols]).astype(bf16)
        grad_n = grad_gn[:, cols]
        ggain_out[:, cols] = jnp.sum(grad_n * normal, axis=0, keepdims=True)
        grad_gated = scale * (grad_n * gain[:, cols]) - pull * gated
        gate_f = gate[:, cols].astype(f32)
        sig = jax.nn.sigmoid(gate_f)
        mixer = g_out[:, cols].astype(f32)
        grad_gate_out[:, cols] = (
            grad_gated * mixer * (sig * (1.0 + gate_f * (1.0 - sig)))
        ).astype(bf16)
        g_low = (grad_gated * (gate_f * sig)).astype(bf16)
        g_out[:, cols] = g_low
        g_f = g_low.astype(f32)
        g_grown = (g_f * spread_pair(grown_v, p, first)).astype(bf16)
        adjoint_out[cols, :] = dot(g_grown, c_rows, (0, 0)).astype(bf16)
        dc_total = dc_total + dot(g_grown, carry[cols, :])
        skip_out[:, cols] = jnp.sum(g_f * act[:, cols].astype(f32), axis=0, keepdims=True)
        term = g_f * ystate_s[:, cols]
        for k in range(2):
            part = jnp.sum(jnp.where(first == (k == 0), term, 0.0), axis=1, keepdims=True)
            row_total = row_total + jnp.where(head_col == 2 * p + k, part, 0.0)
    dc_out[...] = dc_total
    row_out[...] = row_total


def inner_back_kernel(act, xw, g, cum, cum_t, u_out, dbc_out):
    rows = act.shape[0]
    first = low_lanes(rows)
    causal = causal_mask(rows)
    b_rows, c_rows = act[:, INNER : INNER + STATE], act[:, INNER + STATE :]
    scores = dot(c_rows, b_rows, (1, 1))
    cum_v, cum_rows = cum[...], cum_t[...]
    grad_scores = jnp.zeros((rows, rows), f32)
    zero = jnp.zeros((rows, PAIR), bf16)
    for p in range(PAIRS):
        cols = pair_columns(p)
        both = []
        for k in range(2):
            decays = decay_matrix(cum_v, cum_rows, 2 * p + k, causal)
            weights = (decays * scores).astype(bf16)
            both.append(dot(weights, g[:, cols], (0, 0)))
            own = jnp.where(first == (k == 0), g[:, cols], zero)
            grad_scores = grad_scores + decays * dot(own, xw[:, cols], (1, 1))
        u_out[:, cols] = jnp.where(first, both[0], both[1])
    low = grad_scores.astype(bf16)
    dbc_out[:, :STATE] = dot(low, c_rows, (0, 0))
    dbc_out[:, STATE:] = dot(low, b_rows)


def outer_back_kernel(
    act, xw, xs, g, inner, u_inner, adjoint, step, tail, skip, dbc, dc_state,
    grad_act_out, diff_out, col_out, direct_out, term_s, col_s, direct_s,
):
    rows = act.shape[0]
    first = low_lanes(rows)
    step_v, tail_v = step[...], tail[...]
    b_rows = act[:, INNER : INNER + STATE]
    db_total = dbc[:, :STATE]
    for p in range(PAIRS):
        cols = pair_columns(p)
        x_f = act[:, cols].astype(f32)
        g_f = g[:, cols].astype(f32)
        step_b = spread_pair(step_v, p, first)
        u_state = dot(b_rows, adjoint[cols, :], (1, 1)) * spread_pair(tail_v, p, first)
        u_in = u_inner[:, cols]
        u_all = u_in + u_state
        grad_act_out[:, cols] = (step_b * u_all + skip[:, cols] * g_f).astype(bf16)
        term_s[:, cols] = g_f * inner[:, cols] - xw[:, cols].astype(f32) * u_in
        col_s[:, cols] = step_b * x_f * u_state
        direct_s[:, cols] = x_f * u_all
        db_total = db_total + dot(xs[:, cols], adjoint[cols, :])
    grad_act_out[:, INNER : INNER + STATE] = db_total.astype(bf16)
    grad_act_out[:, INNER + STATE :] = (dbc[:, STATE:] + dc_state[...]).astype(bf16)
    selector = head_selector()
    diff_out[...] = dot(term_s[...], selector, precision=highest)
    col_out[...] = dot(col_s[...], selector, precision=highest)
    direct_out[...] = dot(direct_s[...], selector, precision=highest)


def shifted(value, axis, by):
    length = lax.axis_size(axis)
    pairs = [(i, i + by) for i in range(length) if 0 <= i + by < length]
    return lax.ppermute(value, axis, pairs)


def exchange(value):
    return lax.all_to_all(value, SEQ_AXES, split_axis=0, concat_axis=0, tiled=True)


def running(parts, factors, reverse):
    count = parts.shape[0]
    order = range(count - 1, -1, -1) if reverse else range(count)
    state = jnp.zeros(parts.shape[1:], f32)
    kept = [None] * count
    for i in order:
        kept[i] = state.astype(bf16)
        state = factors[i][:, None] * state + parts[i].astype(f32)
    return jnp.stack(kept)


def reduce_weight(part):
    shard = lax.psum_scatter(part.astype(bf16), WEIGHT_AXES, scatter_dimension=0, tiled=True)
    return jnp.sum(lax.all_gather(shard, "head").astype(f32), axis=0)


def body(
    hidden,
    norm_gain,
    in_weight,
    conv_weight,
    conv_bias,
    dt_bias,
    a_log,
    skip_gain,
    gate_gain,
    out_weight,
    cotangent,
):
    rows = hidden.shape[0]
    places = lax.axis_size(SEQ_AXES)
    place = lax.axis_index(SEQ_AXES)
    weight_conv = lax.all_gather(in_weight[:, INNER:], WEIGHT_AXES, axis=0, tiled=True)
    before = shifted(hidden[rows - HALO :], SEQ_AXES, 1)
    weight_gate = lax.all_gather(in_weight[:, :INNER], WEIGHT_AXES, axis=0, tiled=True)
    weight_out = lax.all_gather(out_weight, WEIGHT_AXES, axis=0, tiled=True)

    extended_f = jnp.concatenate([before, hidden], axis=0).astype(f32)
    variance = jnp.mean(extended_f * extended_f, axis=-1, keepdims=True)
    r1 = lax.rsqrt(variance + epsilon)
    normed_ext = (extended_f * r1 * norm_gain).astype(bf16)
    hidden_f, r1, normed_low = extended_f[HALO:], r1[HALO:], normed_ext[HALO:]

    projected = dot(normed_ext, weight_conv).astype(bf16)
    extended = projected[HALO - (CONV - 1) :, :CONV_CH].astype(f32)
    dt_in = projected[HALO:, CONV_CH:].astype(f32) + dt_bias
    conv_out = conv_bias + conv_weight[0] * extended[0:rows]
    for k in range(1, CONV):
        conv_out = conv_out + conv_weight[k] * extended[k : k + rows]
    act = (conv_out * jax.nn.sigmoid(conv_out)).astype(bf16)

    row_ids = lax.broadcasted_iota(jnp.int32, (rows, rows), 0)
    col_ids = lax.broadcasted_iota(jnp.int32, (rows, rows), 1)
    lower = (col_ids <= row_ids).astype(f32)
    rate = jnp.exp(a_log)
    step = jax.nn.softplus(dt_in)
    log_decay = -step * rate
    cum = dot(lower, log_decay, precision=highest)
    last = cum[rows - 1 :]
    tail = jnp.exp(last - cum)
    grown = jnp.exp(cum)
    cum_t = cum.T
    skip_wide = jnp.repeat(skip_gain, HEADDIM)[None]

    xw, xs, state = call(
        state_kernel,
        [((rows, INNER), bf16), ((rows, INNER), bf16), ((INNER, STATE), bf16)],
        act, step, tail,
    )
    share = INNER // places
    high = last.astype(bf16)
    rest = last - high.astype(f32)
    middle = rest.astype(bf16)
    lowest = (rest - middle.astype(f32)).astype(bf16)
    logs = jnp.pad(jnp.concatenate([high, middle, lowest], axis=0), ((0, 13), (0, STATE - HEADS)))
    sent = jnp.concatenate(
        [state.reshape(places, share, STATE), jnp.broadcast_to(logs, (places, 16, STATE))], axis=1
    )
    arrived = exchange(sent)
    inner = call(inner_kernel, [((rows, INNER), f32)], act, xw, cum, cum_t)[0]
    gate = dot(normed_low, weight_gate).astype(bf16)
    grad_gn = dot(cotangent, weight_out, (1, 1))

    all_logs = jnp.sum(arrived[:, share : share + 3, :HEADS].astype(f32), axis=1)
    owner = (place * share + jnp.arange(share)) // HEADDIM
    mine = (owner[None] == jnp.arange(HEADS)[:, None]).astype(f32)
    factors = dot(jnp.exp(all_logs), mine, precision=highest)
    carry = exchange(running(arrived[:, :share], factors, False)).reshape(INNER, STATE)

    middle_outs = [
        ((rows, INNER), bf16),
        ((rows, INNER), bf16),
        ((rows, INNER), bf16),
        ((INNER, STATE), bf16),
        ((1, INNER), f32),
        ((1, INNER), f32),
        ((rows, 128), f32),
        ((rows, STATE), f32),
    ]
    whole = pl.BlockSpec(memory_space=pltpu.VMEM)
    gated_low, grad_gate, g, adjoint_part, ggain, gskip, row_state, dc_state = pl.pallas_call(
        middle_kernel,
        out_shape=[jax.ShapeDtypeStruct(s, d) for s, d in middle_outs],
        in_specs=[whole] * 8,
        out_specs=[whole] * 8,
        scratch_shapes=[pltpu.VMEM((rows, INNER), f32)] * 2,
        compiler_params=pltpu.CompilerParams(vmem_limit_bytes=48 * 1024 * 1024),
    )(act, inner, carry, grown, skip_wide, gate, gate_gain[None], grad_gn)

    arrived_back = exchange(adjoint_part.reshape(places, share, STATE))
    grad_out_weight = reduce_weight(dot(gated_low, cotangent, (0, 0)))
    grad_in_gate = reduce_weight(dot(normed_low, grad_gate, (0, 0)))
    output = (hidden_f + dot(gated_low, weight_out)).astype(bf16)
    u_inner, dbc = call(
        inner_back_kernel,
        [((rows, INNER), f32), ((rows, 2 * STATE), f32)],
        act, xw, g, cum, cum_t,
    )
    adjoint = exchange(running(arrived_back, factors, True)).reshape(INNER, STATE)
    grad_act, diff, col_state, direct = pl.pallas_call(
        outer_back_kernel,
        out_shape=[
            jax.ShapeDtypeStruct((rows, CONV_CH), bf16),
            jax.ShapeDtypeStruct((rows, 128), f32),
            jax.ShapeDtypeStruct((rows, 128), f32),
            jax.ShapeDtypeStruct((rows, 128), f32),
        ],
        in_specs=[whole] * 12,
        out_specs=[whole] * 4,
        scratch_shapes=[pltpu.VMEM((rows, INNER), f32)] * 3,
        compiler_params=pltpu.CompilerParams(vmem_limit_bytes=48 * 1024 * 1024),
    )(act, xw, xs, g, inner, u_inner, adjoint, step, tail, skip_wide, dbc, dc_state)

    sig = jax.nn.sigmoid(conv_out)
    grad_conv = grad_act.astype(f32) * (sig * (1.0 + conv_out * (1.0 - sig)))
    after = shifted(grad_conv[:HALO], SEQ_AXES, -1)
    across = jnp.exp(last[0]) * jnp.sum(
        (adjoint.astype(f32) * carry.astype(f32)).reshape(HEADS, HEADDIM * STATE), axis=1
    )
    upper = (col_ids >= row_ids).astype(f32)
    strict = (col_ids < row_ids).astype(f32)
    grad_log = (
        dot(upper, (diff + row_state)[:, :HEADS], precision=highest)
        + dot(strict, col_state[:, :HEADS], precision=highest)
        + across
    )
    grad_dt = (direct[:, :HEADS] - rate * grad_log) * jax.nn.sigmoid(dt_in)
    grad_a_log = jnp.sum(grad_log * log_decay, axis=0)
    grad_dt_bias = jnp.sum(grad_dt, axis=0)
    grad_skip = jnp.sum(gskip.reshape(HEADS, HEADDIM), axis=1)

    grad_ext = jnp.concatenate([grad_conv, after], axis=0)
    grad_conv_in = conv_weight[CONV - 1] * grad_ext[0:rows]
    for k in range(CONV - 1):
        grad_conv_in = grad_conv_in + conv_weight[k] * grad_ext[CONV - 1 - k : CONV - 1 - k + rows]
    grad_cb = jnp.sum(grad_conv, axis=0)
    grad_cw = jnp.stack(
        [jnp.sum(grad_conv * extended[k : k + rows], axis=0) for k in range(CONV)]
    )
    grad_rest = jnp.concatenate([grad_conv_in, grad_dt], axis=1).astype(bf16)
    grad_in_rest = reduce_weight(dot(normed_low, grad_rest, (0, 0)))
    grad_normed = dot(grad_gate, weight_gate, (1, 1)) + dot(grad_rest, weight_conv, (1, 1))
    pulled = grad_normed * norm_gain
    grad_hidden = (
        cotangent.astype(f32)
        + r1 * pulled
        - r1 * r1 * r1 * hidden_f * jnp.mean(pulled * hidden_f, axis=-1, keepdims=True)
    )
    grad_ngain = jnp.sum(grad_normed * hidden_f * r1, axis=0)
    grad_in_weight = jnp.concatenate([grad_in_gate, grad_in_rest], axis=1)
    small = [grad_ngain, grad_cw.reshape(-1), grad_cb, grad_dt_bias, grad_a_log, grad_skip, ggain[0]]
    packed = jnp.concatenate(small)
    size = packed.shape[0]
    packed = jnp.pad(packed, (0, -size % 1024)).reshape(-1, 128)
    total = jnp.sum(lax.all_gather(packed, ("dp", "ctx", "head")), axis=0).reshape(-1)
    sums, start = [], 0
    for part in small:
        sums.append(total[start : start + part.shape[0]])
        start += part.shape[0]
    return (
        output,
        grad_hidden,
        sums[0],
        grad_in_weight,
        sums[1].reshape(CONV, CONV_CH),
        sums[2],
        sums[3],
        sums[4],
        sums[5],
        sums[6],
        grad_out_weight,
    )


def solution(mesh):
    return jax.shard_map(
        body,
        mesh=mesh,
        in_specs=(
            P(("dp", "ctx", "head"), None),
            P(),
            P(("dp", "ctx"), None),
            P(),
            P(),
            P(),
            P(),
            P(),
            P(),
            P(("dp", "ctx"), None),
            P(("dp", "ctx", "head"), None),
        ),
        out_specs=(
            P(("dp", "ctx", "head"), None),
            P(("dp", "ctx", "head"), None),
            P(),
            P(("dp", "ctx"), None),
            P(),
            P(),
            P(),
            P(),
            P(),
            P(),
            P(("dp", "ctx"), None),
        ),
        check_vma=False,
    )
```

time: 804 us -> 433 us (0.54); the launches traced: 794 us -> 431 us
  local copies, waits for them, and re-layouts: 165 us -> 24.9 us
  matrix products: 160 us -> 32.7 us
  other arithmetic: 125 us -> 36.2 us
  blocking collectives: 59.3 us -> 0 us
  waiting for transfers between devices: 234 us -> 277 us
  Pallas kernels: 0 us -> 21.9 us
  starting transfers between devices: 32.2 us -> 23.7 us
    all_gather x2 -> x7, waiting for transfers between devices: 44.9 us -> 188 us  [the longest x3 89.8 us: reduce_weight(): return jnp.sum(lax.all_gather(shard, 'head').astype(f32), axis=0)]
    dot_general x68 -> x13, matrix products: 160 us -> 32.7 us  [dot(): lax.dot_general(a, b, (((dims[0],), (dims[1],)), ((), ())), preferred_ele...]
    dynamic_update_slice x54 -> x0, local copies, waits for them, and re-layouts: 75 us -> none  [the longest x52 74.6 us: segment_scan(): last_state, outputs = lax.scan(block_math, first_state, pieces)]
    another operation x39 -> x3, other arithmetic: 53.8 us -> 2.53 us
    reduce_scatter x3, waiting for transfers between devices: 102 us -> 58.2 us  [reduce_weight(): lax.psum_scatter(part.astype(bf16), WEIGHT_AXES, scatter_dimension=0, til...]
    psum x1 -> x0, blocking collectives: 43 us -> none  [body(): lax.psum((grad_ngain, grad_cw, grad_cb, place_heads(grad_parts[4], head_f...]
    psum x1 -> x0, waiting for transfers between devices: 29.2 us -> none  [body(): lax.psum((grad_in_shard, grad_out_shard), 'head')]
    all_to_all x6 -> x4, waiting for transfers between devices: 51.4 us -> 26.9 us  [exchange(): lax.all_to_all(value, SEQ_AXES, split_axis=0, concat_axis=0, tiled=True)]
  transfers between devices with their start and end apart: 14 -> 16, of which waited for: 10 -> 13; matrix products, arithmetic and copies ran while one was open for 34% -> 17% of each run, Pallas kernels for 0% -> 3%
where the time goes in v1:
time: 433 us; the launch traced here: 431 us
  waiting for transfers between devices  277 us (64%)
  other arithmetic  36.2 us (8%)
  matrix products  32.7 us (8%)
  local copies, waits for them, and re-layouts  24.9 us (6%)
  starting transfers between devices  23.7 us (5%)
  Pallas kernels  21.9 us (5%)
  between operations  15.1 us (3%)
    all_gather x3, waiting for transfers between devices, reduce_weight(): return jnp.sum(lax.all_gather(shard, 'head').astype(f32), axis=0)  89.8 us
    reduce_scatter x3, waiting for transfers between devices, reduce_weight(): lax.psum_scatter(part.astype(bf16), WEIGHT_AXES, scatter_dimension=0, til...  58.2 us
    all_gather x1, waiting for transfers between devices, body(): lax.all_gather(packed, ('dp', 'ctx', 'head'))  54 us
    dot_general x13, matrix products, dot(): lax.dot_general(a, b, (((dims[0],), (dims[1],)), ((), ())), preferred_ele...  32.7 us
    all_to_all x4, waiting for transfers between devices, exchange(): lax.all_to_all(value, SEQ_AXES, split_axis=0, concat_axis=0, tiled=True)  26.9 us
    all_gather x1, waiting for transfers between devices, body(): lax.all_gather(in_weight[:, INNER:], WEIGHT_AXES, axis=0, tiled=True)  26.7 us
    all_gather x1, waiting for transfers between devices, body(): weight_out = lax.all_gather(out_weight, WEIGHT_AXES, axis=0, tiled=True)  17.8 us
    all_to_all x4, starting transfers between devices, exchange(): lax.all_to_all(value, SEQ_AXES, split_axis=0, concat_axis=0, tiled=True)  16.3 us
  transfers between devices with their start and end apart: 16, of which 13 were waited for; matrix products, arithmetic and copies ran while one was open for 17% of the time, Pallas kernels for 3%

profile of v1, /device:TPU:0, one launch (start us, length us, event | category | flops | bytes accessed | tf_op | source)
XLA Modules:
  0.0 431.2 jit_solution(8872014205639621757)
XLA Ops:
  11.0 4.9 %collective-permute-start = (bf16[8,768]{1,0:T(8,128)(2,1)S(1)}, bf16[8,768]{1,0:T(8,128)(2,1)S(1)}, u32[]{:S(2)}, u32[]{:S(2)}) collective-permute-start(bf16[8,768]{1,0:T(8,128)(2,1)S(1)} %slice.206), channel_id=1, source_target_pairs={{0,1},{1,2},{2,3},{3,4},{4,5},{5,6},{6,7},{8,9},{9,10},{10,11},{11... | collective-permute-start | bytes 36872 | tf_op jit(solution)/shard_map/ppermute | solution.py:216
  18.1 26.7 %all-gather.11.cloned.1.call-done = bf16[768,1816]{1,0:T(8,128)(2,1)} async-done(((bf16[96,1816]{1,0:T(8,128)(2,1)}), bf16[768,1816]{1,0:T(8,128)(2,1)}) %all-gather.11.cloned.1.call-update) | async-done | bytes 2789392 | tf_op jit(solution)/shard_map/all_gather | solution.py:255
  44.7 2.9 convolution_convert_fusion.3
  49.9 5.9 %multiply_convert_fusion = (bf16[256,1792]{1,0:T(8,128)(2,1)S(1)}, f32[256,1792]{1,0:T(8,128)}) fusion(f32[259,1792]{1,0:T(8,128)} %slice_convert_fusion, f32[1792]{0:T(1024)S(1)} %get-tuple-element.54, f32[1792]{0:T(1024)S(1)} %get-tuple-element.55, f32[1792]{0:T(1024)S(1)} %get-tuple-element.53, f32[1792]{0:T(1024)S(1)} %get-tuple-element.52, ...), kind=kLoop, calls=%fused_computation.25 | loop fusion | flops 5963776 | bytes 10128384 | tf_op jit(solution)/shard_map/convert_element_type | solution.py:272
  55.7 2.8 shard_map.194
  60.2 4.7 %all-to-all-start = ((bf16[8,208,128]{2,1,0:T(8,128)(2,1)}), bf16[8,208,128]{2,1,0:T(8,128)(2,1)S(1)}, u32[]{:S(2)}, u32[]{:S(2)}) async-start(bf16[8,208,128]{2,1,0:T(8,128)(2,1)} %pad_maximum_fusion.5), calls=%async_computation | async-start | bytes 851968 | tf_op jit(solution)/shard_map/all_to_all | solution.py:220
  65.0 12.8 %all-to-all-done = bf16[8,208,128]{2,1,0:T(8,128)(2,1)S(1)} async-done(((bf16[8,208,128]{2,1,0:T(8,128)(2,1)}), bf16[8,208,128]{2,1,0:T(8,128)(2,1)S(1)}, u32[]{:S(2)}, u32[]{:S(2)}) %all-to-all-start) | async-done | bytes 426016 | tf_op jit(solution)/shard_map/all_to_all | solution.py:220
  82.1 3.5 all-to-all-start.1
  86.1 3.4 convolution_convert_fusion.4.gate
  89.4 17.8 %all-gather.15.cloned.1.call-done = bf16[1536,768]{1,0:T(8,128)(2,1)} async-done(((bf16[192,768]{1,0:T(8,128)(2,1)}), bf16[1536,768]{1,0:T(8,128)(2,1)}) %all-gather.15.cloned.1.call-update) | async-done | bytes 2359312 | tf_op jit(solution)/shard_map/all_gather | solution.py:258
  107.2 3.6 fusion.56.grad_gn
  114.8 7.4 %shard_map.196 = (bf16[256,1536]{1,0:T(8,128)(2,1)S(1)}, bf16[256,1536]{1,0:T(8,128)(2,1)S(1)}, bf16[256,1536]{1,0:T(8,128)(2,1)S(1)}, bf16[1536,128]{1,0:T(8,12...) custom-call(bf16[256,1792]{1,0:T(8,128)(2,1)S(1)} %get-tuple-element.6, ...), custom_call_target="tpu_custom_call" | custom-call | tf_op jit(solution)/shard_map/pallas_call | solution.py:323
  125.3 2.3 convolution_convert_fusion.2
  127.6 4.6 %all-to-all-start.2 = ((bf16[8,192,128]{2,1,0:T(8,128)(2,1)}), bf16[8,192,128]{2,1,0:T(8,128)(2,1)S(1)}, u32[]{:S(2)}, u32[]{:S(2)}) async-start(bf16[8,192,128]{2,1,0:T(8,128)(2,1)} %bitcast.12), calls=%async_computation.2 | async-start | bytes 786432 | tf_op jit(solution)/shard_map/all_to_all | solution.py:220
  132.3 3.6 convolution_convert_fusion
  135.9 8.4 %all-to-all-done.2 = bf16[8,192,128]{2,1,0:T(8,128)(2,1)S(1)} async-done(((bf16[8,192,128]{2,1,0:T(8,128)(2,1)}), bf16[8,192,128]{2,1,0:T(8,128)(2,1)S(1)}, u32[]{:S(2)}, u32[]{:S(2)}) %all-to-all-start.2) | async-done | bytes 393248 | tf_op jit(solution)/shard_map/all_to_all | solution.py:220
  154.3 3.5 all-to-all-start.3
  158.8 3.3 shard_map.197
  164.0 5.8 %all-to-all-done.3 = bf16[8,192,128]{2,1,0:T(8,128)(2,1)S(1)} async-done(((bf16[8,192,128]{2,1,0:T(8,128)(2,1)}), bf16[8,192,128]{2,1,0:T(8,128)(2,1)S(1)}, u32[]{:S(2)}, u32[]{:S(2)}) %all-to-all-start.3) | async-done | bytes 393248 | tf_op jit(solution)/shard_map/all_to_all | solution.py:220
  176.0 6.9 %shard_map.198 = (bf16[256,1792]{1,0:T(8,128)(2,1)S(1)}, f32[256,128]{1,0:T(8,128)S(1)}, f32[256,128]{1,0:T(8,128)S(1)}, f32[256,128]{1,0:T(8,128)S(1)}) custom-call(bf16[256,1792]{1,0:T(8,128)(2,1)S(1)} %get-tuple-element.63.act, bf16[256,1536]{1,0:T(8,128)(2,1)S(1)} %get-tuple-element.28.xw, bf16[256,1536]{1,0:T(8,128)(2,1)S(1)} %copy-done.10, ...), custom_call_target="tpu_custom_call" | custom-call | tf_op jit(solution)/shard_map/pallas_call | solution.py:342
  183.0 2.3 multiply_reduce_fusion.3
  193.4 2.6 convolution_convert_fusion.1
  197.4 3.4 fusion.57
  201.0 4.1 multiply_reduce_fusion.5
  206.7 9.7 %reduce-scatter.8.cloned.1.call-done = bf16[192,768]{1,0:T(8,128)(2,1)} async-done(((bf16[1536,768]{1,0:T(8,128)(2,1)}), bf16[192,768]{1,0:T(8,128)(2,1)}) %reduce-scatter.8.cloned.1.call-update) | async-done | bytes 294928 | tf_op jit(solution)/shard_map/reduce_scatter | solution.py:235
  216.4 48.5 %reduce-scatter.6.cloned.1.call-done = bf16[96,1816]{1,0:T(8,128)(2,1)} async-done(((bf16[768,1816]{1,0:T(8,128)(2,1)}), bf16[96,1816]{1,0:T(8,128)(2,1)}) %reduce-scatter.6.cloned.1.call-update) | async-done | bytes 348688 | tf_op jit(solution)/shard_map/reduce_scatter | solution.py:235
  264.9 3.3 fusion.9
  269.4 54.0 %all-gather.17.cloned.1.call-done = f32[32,96,128]{2,1,0:T(8,128)} async-done(((f32[1,96,128]{2,1,0:T(8,128)}), f32[32,96,128]{2,1,0:T(8,128)}) %all-gather.17.cloned.1.call-update) | async-done | bytes 1572880 | tf_op jit(solution)/shard_map/all_gather | solution.py:397
  328.0 26.4 %all-gather.19.cloned.1.call-done = bf16[384,1536]{1,0:T(8,128)(2,1)} async-done(((bf16[96,1536]{1,0:T(8,128)(2,1)}), bf16[384,1536]{1,0:T(8,128)(2,1)}) %all-gather.19.cloned.1.call-update) | async-done | bytes 1179664 | tf_op jit(solution)/shard_map/all_gather | solution.py:236
  355.8 29.7 %all-gather.23.cloned.1.call-done = bf16[768,768]{1,0:T(8,128)(2,1)} async-done(((bf16[192,768]{1,0:T(8,128)(2,1)}), bf16[768,768]{1,0:T(8,128)(2,1)}) %all-gather.23.cloned.1.call-update) | async-done | bytes 1179664 | tf_op jit(solution)/shard_map/all_gather | solution.py:236
  385.5 2.3 convert_reduce_fusion.1
  387.8 33.7 %all-gather.21.cloned.1.call-done = bf16[384,1816]{1,0:T(8,128)(2,1)} async-done(((bf16[96,1816]{1,0:T(8,128)(2,1)}), bf16[384,1816]{1,0:T(8,128)(2,1)}) %all-gather.21.cloned.1.call-update) | async-done | bytes 1394704 | tf_op jit(solution)/shard_map/all_gather | solution.py:236
  (245 shorter events, 61.6 us)
Async XLA Ops:
  7.2 8.8 %copy-start.68 = (f32[24]{0:T(128)S(1)}, f32[24]{0:T(128)}, u32[]{:S(2)}) copy-start(f32[24]{0:T(128)} %param.17) | copy-start | bytes 292
  7.2 10.3 %copy-start.55 = (f32[768]{0:T(1024)S(1)}, f32[768]{0:T(1024)}, u32[]{:S(2)}) copy-start(f32[768]{0:T(1024)} %param.12) | copy-start | bytes 9220
  7.2 37.5 %all-gather.11.cloned.1.call-start = ((), (), s32[]{:S(2)}) async-start(), calls=%async_computation.7 | async-start | bytes 3317760 | tf_op jit(solution)/shard_map/all_gather | solution.py:255
  9.1 76.9 %all-gather.13.cloned.1.call-start = ((), (), s32[]{:S(2)}) async-start(), calls=%async_computation.8 | async-start | bytes 2654208 | tf_op jit(solution)/shard_map/all_gather | solution.py:257
  10.9 96.3 %all-gather.15.cloned.1.call-start = ((), (), s32[]{:S(2)}) async-start(), calls=%async_computation.9 | async-start | bytes 2654208 | tf_op jit(solution)/shard_map/all_gather | solution.py:258
  11.0 6.3 %collective-permute-start = (bf16[8,768]{1,0:T(8,128)(2,1)S(1)}, bf16[8,768]{1,0:T(8,128)(2,1)S(1)}, u32[]{:S(2)}, u32[]{:S(2)}) collective-permute-start(bf16[8,768]{1,0:T(8,128)(2,1)S(1)} %slice.206), channel_id=1, source_target_pairs={{0,1},{1,2},{2,3},{3,4},{4,5},{5,6},{6,7},{8,9},{9,10},{10,11},{11... | collective-permute-start | bytes 36872 | tf_op jit(solution)/shard_map/ppermute | solution.py:216
  16.0 33.8 %copy-start.38 = (f32[1792]{0:T(1024)}, f32[1792]{0:T(1024)S(1)}, u32[]{:S(2)}) copy-start(f32[1792]{0:T(1024)S(1)} %get-tuple-element.52) | copy-start | bytes 21508
  16.0 33.8 %copy-start.40 = (f32[1792]{0:T(1024)}, f32[1792]{0:T(1024)S(1)}, u32[]{:S(2)}) copy-start(f32[1792]{0:T(1024)S(1)} %get-tuple-element.53) | copy-start | bytes 21508
  16.0 33.8 %copy-start.42 = (f32[1792]{0:T(1024)}, f32[1792]{0:T(1024)S(1)}, u32[]{:S(2)}) copy-start(f32[1792]{0:T(1024)S(1)} %get-tuple-element.54) | copy-start | bytes 21508
  16.1 33.8 %copy-start.44 = (f32[1792]{0:T(1024)}, f32[1792]{0:T(1024)S(1)}, u32[]{:S(2)}) copy-start(f32[1792]{0:T(1024)S(1)} %get-tuple-element.55) | copy-start | bytes 21508
  16.1 33.1 %copy-start.69 = (f32[24]{0:T(128)}, f32[24]{0:T(128)S(1)}, u32[]{:S(2)}) copy-start(f32[24]{0:T(128)S(1)} %exp.29) | copy-start | bytes 292
  18.1 68.0 %copy-start.26 = (bf16[264,768]{1,0:T(8,128)(2,1)}, bf16[264,768]{1,0:T(8,128)(2,1)S(1)}, u32[]{:S(2)}) copy-start(bf16[264,768]{1,0:T(8,128)(2,1)S(1)} %multiply_convert_fusion.1) | copy-start | bytes 1216516
  49.6 61.4 %copy-start.13 = (f32[256,24]{0,1:T(8,128)}, f32[256,24]{0,1:T(8,128)S(1)}, u32[]{:S(2)}) copy-start(f32[256,24]{0,1:T(8,128)S(1)} %get-tuple-element.81) | copy-start | bytes 73732
  60.2 25.6 %copy-start.67 = (f32[24]{0:T(128)S(1)}, f32[24]{0:T(128)}, u32[]{:S(2)}) copy-start(f32[24]{0:T(128)} %param.18) | copy-start | bytes 292
  60.2 25.8 %copy-start.61 = (f32[1536]{0:T(1024)S(1)}, f32[1536]{0:T(1024)}, u32[]{:S(2)}) copy-start(f32[1536]{0:T(1024)} %param.19) | copy-start | bytes 18436
  60.2 17.5 %all-to-all-start = ((bf16[8,208,128]{2,1,0:T(8,128)(2,1)}), bf16[8,208,128]{2,1,0:T(8,128)(2,1)S(1)}, u32[]{:S(2)}, u32[]{:S(2)}) async-start(bf16[8,208,128]{2,1,0:T(8,128)(2,1)} %pad_maximum_fusion.5), calls=%async_computation | async-start | bytes 851968 | tf_op jit(solution)/shard_map/all_to_all | solution.py:220
  78.5 11.0 %copy-start.57 = (f32[1,192]{1,0:T(1,128)}, f32[1,192]{1,0:T(1,128)S(1)}, u32[]{:S(2)}) copy-start(f32[1,192]{1,0:T(1,128)S(1)} %get-tuple-element.75) | copy-start | bytes 2308
  78.5 10.9 %copy-start.58 = (f32[1,192]{1,0:T(1,128)}, f32[1,192]{1,0:T(1,128)S(1)}, u32[]{:S(2)}) copy-start(f32[1,192]{1,0:T(1,128)S(1)} %get-tuple-element.76) | copy-start | bytes 2308
  82.1 31.5 %all-to-all-start.1 = ((bf16[8,192,128]{2,1,0:T(8,128)(2,1)}), bf16[8,192,128]{2,1,0:T(8,128)(2,1)S(1)}, u32[]{:S(2)}, u32[]{:S(2)}) async-start(bf16[8,192,128]{2,1,0:T(8,128)(2,1)} %fusion.34), calls=%async_computation.1 | async-start | bytes 786432 | tf_op jit(solution)/shard_map/all_to_all | solution.py:220
  85.6 120.3 %reduce-scatter.4.cloned.1.call-start = ((), (), s32[]{:S(2)}) async-start(), calls=%async_computation.11 | async-start | bytes 2654208 | tf_op jit(solution)/shard_map/reduce_scatter | solution.py:235
  86.0 21.2 %copy-start.31 = (bf16[256,768]{1,0:T(8,128)(2,1)S(1)}, bf16[256,768]{1,0:T(8,128)(2,1)}, u32[]{:S(2)}) copy-start(bf16[256,768]{1,0:T(8,128)(2,1)} %param.21) | copy-start | bytes 1179652
  114.8 10.5 %copy-start.27 = (bf16[264,768]{1,0:T(8,128)(2,1)S(1)}, bf16[264,768]{1,0:T(8,128)(2,1)}, u32[]{:S(2)}) copy-start(bf16[264,768]{1,0:T(8,128)(2,1)} %copy-done.26) | copy-start | bytes 1216516
  127.6 16.7 %all-to-all-start.2 = ((bf16[8,192,128]{2,1,0:T(8,128)(2,1)}), bf16[8,192,128]{2,1,0:T(8,128)(2,1)S(1)}, u32[]{:S(2)}, u32[]{:S(2)}) async-start(bf16[8,192,128]{2,1,0:T(8,128)(2,1)} %bitcast.12), calls=%async_computation.2 | async-start | bytes 786432 | tf_op jit(solution)/shard_map/all_to_all | solution.py:220
  132.3 84.1 %reduce-scatter.8.cloned.1.call-start = ((), (), s32[]{:S(2)}) async-start(), calls=%async_computation.13 | async-start | bytes 2654208 | tf_op jit(solution)/shard_map/reduce_scatter | solution.py:235
  154.3 15.5 %all-to-all-start.3 = ((bf16[8,192,128]{2,1,0:T(8,128)(2,1)}), bf16[8,192,128]{2,1,0:T(8,128)(2,1)S(1)}, u32[]{:S(2)}, u32[]{:S(2)}) async-start(bf16[8,192,128]{2,1,0:T(8,128)(2,1)} %constant_dynamic-update-slice_fusion.1), calls=%async_computation.3 | async-start | bytes 786432 | tf_op jit(solution)/shard_map/all_to_all | solution.py:220
  157.8 107.1 %reduce-scatter.6.cloned.1.call-start = ((), (), s32[]{:S(2)}) async-start(), calls=%async_computation.12 | async-start | bytes 3317760 | tf_op jit(solution)/shard_map/reduce_scatter | solution.py:235
  185.3 6.3 %collective-permute-start.1 = (f32[8,1792]{1,0:T(8,128)S(1)}, f32[8,1792]{1,0:T(8,128)}, u32[]{:S(2)}, u32[]{:S(2)}) collective-permute-start(f32[8,1792]{1,0:T(8,128)S(1)} %slice.301), channel_id=1, source_target_pairs={{1,0},{2,1},{3,2},{4,3},{5,4},{6,5},{7,6},{9,8},{10,9},{11,10},{12... | collective-permute-start | bytes 172040 | tf_op jit(solution)/shard_map/ppermute | solution.py:216
  196.1 127.3 %all-gather.17.cloned.1.call-start = ((), (), s32[]{:S(2)}) async-start(), calls=%async_computation.10 | async-start | bytes 1622016 | tf_op jit(solution)/shard_map/all_gather | solution.py:397
  201.0 63.9 %copy-start.5 = (bf16[256,1536]{1,0:T(8,128)(2,1)S(1)}, bf16[256,1536]{1,0:T(8,128)(2,1)}, u32[]{:S(2)}) copy-start(bf16[256,1536]{1,0:T(8,128)(2,1)} %copy-done.4) | copy-start | bytes 2359300
  205.9 148.5 %all-gather.19.cloned.1.call-start = ((), (), s32[]{:S(2)}) async-start(), calls=%async_computation.14 | async-start | bytes 1474560 | tf_op jit(solution)/shard_map/all_gather | solution.py:236
  206.6 178.9 %all-gather.23.cloned.1.call-start = ((), (), s32[]{:S(2)}) async-start(), calls=%async_computation.16 | async-start | bytes 1474560 | tf_op jit(solution)/shard_map/all_gather | solution.py:236
  216.4 205.2 %all-gather.21.cloned.1.call-start = ((), (), s32[]{:S(2)}) async-start(), calls=%async_computation.15 | async-start | bytes 1843200 | tf_op jit(solution)/shard_map/all_gather | solution.py:236
  (55 other events, 156.1 us)
Sparse Core Ops, SparseCore 0:
  10.5 34.1 all-gather.10
  47.2 29.0 all-gather.12
  78.1 29.0 all-gather.14
  127.7 42.4 reduce-scatter.3
  173.8 42.4 reduce-scatter.7
  219.6 45.2 reduce-scatter.5
  268.3 55.0 all-gather.16
  325.0 29.3 all-gather.18
  355.9 29.5 all-gather.22
  386.9 34.5 all-gather.20
